TPU v7x, 32 devices: a whole 2x2x4 slice. The times are simulated.
32 devices in a mesh: dp: 8 (over y, x, core), tensor: 4 (over z).
Axes of the slice: x: 2, y: 2, z: 4, core: 2. Of those that a mesh axis runs over, the one named last changes fastest.
Arguments:
- learn_hidden: bfloat16 [384, 4096], P('dp', 'tensor'), may hold values from -360 to 360
- target_hidden: bfloat16 [384, 4096], P('dp', 'tensor'), may hold values from -360 to 360
- reward: bfloat16 [384], P('dp'), may hold values from -6 to 6
- learn_head: bfloat16 [4096, 128256], P(None, ('dp', 'tensor')), may hold values from -0.09375 to 0.09375
- target_head: bfloat16 [4096, 128256], P(None, ('dp', 'tensor')), may hold values from -0.09375 to 0.09375
- action: int32 [384], P('dp'), may hold values from 0 to 128255
- traj_len: int32 [16], P('dp'), may hold values from 1 to 24, 288 in all
- owner: int32 [16], P('dp'), may hold values from 0 to 7
Outputs:
- head_grad: bfloat16 [4096, 128256], P(None, ('dp', 'tensor'))
- hidden_grad: bfloat16 [384, 4096], P('dp', 'tensor')
- priority: float32 [8, 24], P('dp')
All inputs are finite; a program needn't handle non-finite values. No bound on the sum of `traj_len` on one device may be relied on, other than what follows from the above.
Results may differ from a plain program's by a relative error of at most 0.005.
Values may be sent and summed in bfloat16 or wider, within the bound.
A program may use at most 192 MiB of HBM per device.

v0:
```python
import jax
import jax.numpy as jnp
from jax import lax
from jax.sharding import PartitionSpec as P

temper = 1.0
discount = 0.99
kl_weight = 10.0


def local_stats(logits):
    row_max = jnp.max(logits, axis=1)
    total = jnp.sum(jnp.exp((logits - row_max[:, None]) / temper), axis=1)
    return (row_max, total)


def shards(learn_hidden, target_hidden, reward, learn_head, target_head, action, traj_len, owner):
    learn_feat, target_feat = (
        lax.all_gather(learn_hidden, "tensor", axis=1, tiled=True),
        lax.all_gather(target_hidden, "tensor", axis=1, tiled=True),
    )
    learn_all, reward_all = (
        lax.all_gather(learn_feat, "dp", axis=0, tiled=True),
        lax.all_gather(reward, "dp", axis=0, tiled=True),
    )
    action_all, length_all, owner_all = (
        lax.all_gather(action, "dp", axis=0, tiled=True),
        lax.all_gather(traj_len, "dp", axis=0, tiled=True),
        lax.all_gather(owner, "dp", axis=0, tiled=True),
    )
    target_q = jnp.dot(
        lax.all_gather(target_feat, "dp", axis=0, tiled=True),
        target_head,
        preferred_element_type=jnp.float32,
    )
    learn_q = jnp.dot(learn_all, learn_head, preferred_element_type=jnp.float32)
    tokens = learn_all.shape[0]
    width = learn_head.shape[1]
    traj_count = length_all.shape[0]
    seq_len = tokens // traj_count
    block_index = lax.axis_index("dp") * lax.axis_size("tensor") + lax.axis_index("tensor")
    columns = block_index * width + jnp.arange(width, dtype=jnp.int32)
    hits = action_all[:, None] == columns[None, :]
    picked_part = jnp.sum(jnp.where(hits, learn_q, 0.0), axis=1)
    learn_peak, learn_part = local_stats(learn_q)
    target_peak, target_part = local_stats(target_q)
    learn_max, target_max = lax.pmax((learn_peak, target_peak), ("dp", "tensor"))
    learn_scaled = learn_part * jnp.exp((learn_peak - learn_max) / temper)
    target_scaled = target_part * jnp.exp((target_peak - target_max) / temper)
    learn_sum, target_sum, picked = lax.psum(
        (learn_scaled, target_scaled, picked_part), ("dp", "tensor")
    )
    target_value = target_max + temper * jnp.log(target_sum)
    learn_p = jnp.exp((learn_q - learn_max[:, None]) / temper) / learn_sum[:, None]
    target_p = jnp.exp((target_q - target_max[:, None]) / temper) / target_sum[:, None]
    position = jnp.arange(tokens, dtype=jnp.int32)
    offset = position % seq_len
    lengths = jnp.repeat(length_all, seq_len)
    live = (offset < lengths).astype(jnp.float32)
    follow = (offset + 1 < lengths).astype(jnp.float32)
    shifted = jnp.concatenate([target_value[1:], jnp.zeros((1,), jnp.float32)])
    target_y = reward_all.astype(jnp.float32) + discount * follow * shifted
    delta = live * (picked - target_y)
    grad_q = (
        jnp.where(hits, delta[:, None], 0.0)
        + kl_weight * live[:, None] * (learn_p - target_p) / temper
    ) / traj_count
    grad_q = grad_q.astype(jnp.bfloat16)
    head_grad = lax.dot_general(
        learn_all, grad_q, (((0,), (0,)), ((), ())), preferred_element_type=jnp.float32
    ).astype(jnp.bfloat16)
    row_sums = lax.psum_scatter(
        lax.dot_general(
            grad_q, learn_head, (((1,), (1,)), ((), ())), preferred_element_type=jnp.float32
        ),
        "dp",
        scatter_dimension=0,
        tiled=True,
    )
    hidden_grad = lax.psum_scatter(row_sums, "tensor", scatter_dimension=1, tiled=True)
    hidden_grad = hidden_grad.astype(jnp.bfloat16)
    owners_all = lax.axis_size("dp")
    magnitude = jnp.abs(delta).reshape(traj_count, seq_len)
    owner_table = (jnp.arange(owners_all, dtype=jnp.int32)[:, None] == owner_all[None, :]).astype(
        jnp.float32
    )
    sums = jnp.dot(owner_table, magnitude, precision=lax.Precision.HIGHEST)
    priority = lax.dynamic_slice_in_dim(sums, lax.axis_index("dp"), 1, 0)
    return (head_grad, hidden_grad, priority)


def solution(mesh):
    return jax.shard_map(
        shards,
        mesh=mesh,
        in_specs=(
            P("dp", "tensor"),
            P("dp", "tensor"),
            P("dp"),
            P(None, ("dp", "tensor")),
            P(None, ("dp", "tensor")),
            P("dp"),
            P("dp"),
            P("dp"),
        ),
        out_specs=(P(None, ("dp", "tensor")), P("dp", "tensor"), P("dp", None)),
        check_vma=False,
    )
```

profile of v0, /device:TPU:0, one launch (start us, length us, event | category | flops | bytes accessed | tf_op | source)
XLA Modules:
  0.0 320.3 jit_solution(17905636004526681801)
XLA Ops:
  7.2 0.0 all-gather.5.cloned.1.call-start
  7.2 18.3 %all_gather.29 = bf16[48,4096]{1,0:T(8,128)(2,1)} all-gather(bf16[48,1024]{1,0:T(8,128)(2,1)} %param.9), channel_id=1, replica_groups=mesh['dp'=8,'tensor'=4] {'tensor'}, dimensions={1}, use_global_device_ids=true | all-gather | bytes 491520 | tf_op jit(solution)/shard_map/all_gather | solution.py:20
  25.5 0.0 all-gather.5.cloned.1.call-update
  25.5 0.0 all-gather.3.cloned.1.call-start
  25.5 15.7 %all_gather.26 = bf16[48,4096]{1,0:T(8,128)(2,1)} all-gather(bf16[48,1024]{1,0:T(8,128)(2,1)} %param.8), channel_id=1, replica_groups=mesh['dp'=8,'tensor'=4] {'tensor'}, dimensions={1}, use_global_device_ids=true | all-gather | bytes 491520 | tf_op jit(solution)/shard_map/all_gather | solution.py:19
  41.2 0.0 reduce-scatter.3.cloned.1.call-start
  41.3 1.2 dynamic-slice
  43.8 0.9 dynamic-update-slice.1
  44.7 0.8 dynamic-update-slice.3
  45.5 0.8 dynamic-update-slice
  46.4 8.1 %all-reduce.4 = (s32[384]{0:T(512)S(1)}, s32[16]{0:T(128)S(1)}, s32[16]{0:T(128)S(1)}) all-reduce(s32[384]{0:T(512)S(1)} %dynamic-update-slice, s32[16]{0:T(128)S(1)} %dynamic-update-slice.1, s32[16]{0:T(128)S(1)} %dynamic-update-slice.3), channel_id=1, replica_groups=mesh['dp'=8,'tensor'=4] {'dp'}, use_global_device_ids=true, to_apply=%add | all-reduce | flops 416 | bytes 3328
  54.5 0.1 broadcast_in_dim.12
  54.6 0.1 reshape.41
  54.7 0.9 dynamic-update-slice.2
  55.6 11.8 %all-reduce.2 = bf16[384]{0:T(512)(128)(2,1)S(1)} all-reduce(bf16[384]{0:T(512)(128)(2,1)S(1)} %dynamic-update-slice.2), channel_id=1, replica_groups=mesh['dp'=8,'tensor'=4] {'dp'}, use_global_device_ids=true, to_apply=%add.2 | all-reduce | flops 384 | bytes 1536
  67.4 22.3 %fusion.18 = (f32[384]{0:T(512)S(1)}, f32[384,4008]{0,1:T(8,128)S(1)}) fusion(bf16[384,4096]{1,0:T(8,128)(2,1)} %all-gather.5.cloned.1.call-done, bf16[4096,4008]{0,1:T(8,128)(2,1)} %param.12), kind=kOutput, calls=%fused_computation.31 | convolution fusion | flops 12609616896 | bytes 42137088 | tf_op jit(solution)/shard_map/dot_general | solution.py:31
  89.7 2.6 copy-done
  92.3 1.0 exponential_reduce_fusion.1
  93.3 23.2 %fusion.19 = (f32[384]{0:T(512)S(1)}, f32[384,4008]{0,1:T(8,128)}) fusion(bf16[384,4096]{1,0:T(8,128)(2,1)} %all-gather.3.cloned.1.call-done, bf16[4096,4008]{0,1:T(8,128)(2,1)} %param.11), kind=kOutput, calls=%fused_computation.32 | convolution fusion | flops 12609616896 | bytes 42137088 | tf_op jit(solution)/shard_map/dot_general | solution.py:36
  116.6 38.1 %all-reduce.6 = (f32[384]{0:T(512)S(1)}, f32[384]{0:T(512)S(1)}) all-reduce(f32[384]{0:T(512)S(1)} %get-tuple-element.16, f32[384]{0:T(512)S(1)} %get-tuple-element.18), channel_id=1, replica_groups=mesh['dp'=8,'tensor'=4] {'dp','tensor'}, use_global_device_ids=true, to_apply=%region_3.4 | all-reduce | flops 768 | bytes 6144 | tf_op jit(solution)/shard_map/pmax | solution.py:47
  154.6 4.5 %fusion = (f32[384]{0:T(512)S(1)}, f32[384]{0:T(512)S(1)}) fusion(f32[384,4008]{0,1:T(8,128)} %get-tuple-element.19, s32[384]{0:T(512)S(1)} %get-tuple-element.5, s32[4008]{0:T(1024)S(1)} %iota_add_fusion, f32[384]{0:T(512)S(1)} %get-tuple-element.18), kind=kLoop, calls=%fused_computation.3 | loop fusion | flops 7694592 | bytes 6178464 | tf_op jit(solution)/shard_map/reduce_sum | solution.py:44
  159.1 41.2 %all-reduce.5 = (f32[384]{0:T(512)S(1)}, f32[384]{0:T(512)S(1)}, f32[384]{0:T(512)S(1)}) all-reduce(f32[384]{0:T(512)S(1)} %get-tuple-element.21, f32[384]{0:T(512)S(1)} %get-tuple-element.20, f32[384]{0:T(512)S(1)} %get-tuple-element.3), channel_id=1, replica_groups=mesh['dp'=8,'tensor'=4] {'dp','tensor'}, use_global_device_ids=true, to_apply=%region_5.6 | all-reduce | flops 1152 | bytes 9216 | tf_op jit(solution)/shard_map/psum | solution.py:50
  200.3 0.1 slice.3
  200.4 0.1 fusion.16
  200.5 23.8 %fusion.13 = f32[384,4096]{1,0:T(8,128)} fusion(bf16[4096,4008]{0,1:T(8,128)(2,1)} %param.11, f32[384,4008]{0,1:T(8,128)} %copy-done, f32[384,4008]{0,1:T(8,128)} %get-tuple-element.19, f32[384]{0:T(512)S(1)} %get-tuple-element.8, f32[384]{0:T(512)S(1)} %get-tuple-element.11, f32[384]{0:T(512)S(1)} %get-tuple-element.9, f32[384]{0:T(512)S(1)} %get-tuple-element.12, ...), kind=kOutput, calls=%fused_computation.29 | convolution fusion | flops 12625007616 | bytes 51464352 | tf_op jit(solution)/shard_map/dot_general | solution.py:73
  224.3 0.0 reduce-scatter.5.cloned.1.call-start
  224.3 0.1 reshape.42
  224.4 0.1 fusion.4
  224.5 0.5 constant_dynamic-slice_fusion
  225.1 61.0 %reduce-scatter.3.cloned.1.call-done = f32[48,4096]{1,0:T(8,128)} async-done(((f32[384,4096]{1,0:T(8,128)}), f32[48,4096]{1,0:T(8,128)}) %reduce-scatter.3.cloned.1.call-update) | async-done | bytes 786448 | tf_op jit(solution)/shard_map/reduce_scatter | solution.py:72
  286.1 26.1 %convert_bitcast_fusion = bf16[4096,4008]{0,1:T(8,128)(2,1)} fusion(bf16[384,4096]{1,0:T(8,128)(2,1)S(1)} %copy-done.1, f32[384,4008]{0,1:T(8,128)} %copy-done, f32[384,4008]{0,1:T(8,128)} %get-tuple-element.19, f32[384]{0:T(512)S(1)} %get-tuple-element.8, f32[384]{0:T(512)S(1)} %get-tuple-element.11, f32[384]{0:T(512)S(1)} %get-tuple-element.9, ...), kind=kOutput, calls=%fused_computation | convolution fusion | flops 12641424384 | bytes 48318624 | tf_op jit(solution)/shard_map/dot_general | solution.py:69
  312.2 1.6 convert_element_type.23
  (16 shorter events, 0.1 us)
Async XLA Ops:
  7.2 60.2 %all-gather.5.cloned.1.call-start = ((), (), s32[]{:S(2)}) async-start(), calls=%async_computation.3 | async-start | bytes 3538944 | tf_op jit(solution)/shard_map/all_gather | solution.py:32
  25.5 67.8 %all-gather.3.cloned.1.call-start = ((), (), s32[]{:S(2)}) async-start(), calls=%async_computation.2 | async-start | bytes 3538944 | tf_op jit(solution)/shard_map/all_gather | solution.py:23
  41.2 244.8 %reduce-scatter.3.cloned.1.call-start = ((), (), s32[]{:S(2)}) async-start(), calls=%async_computation.4 | async-start | bytes 7077888 | tf_op jit(solution)/shard_map/reduce_scatter | solution.py:72
  89.7 2.6 copy-start
  224.3 61.8 %copy-start.1 = (bf16[384,4096]{1,0:T(8,128)(2,1)S(1)}, bf16[384,4096]{1,0:T(8,128)(2,1)}, u32[]{:S(2)}) copy-start(bf16[384,4096]{1,0:T(8,128)(2,1)} %all-gather.3.cloned.1.call-done) | copy-start | bytes 9437188
  224.3 87.9 %reduce-scatter.5.cloned.1.call-start = ((), (), s32[]{:S(2)}) async-start(), calls=%async_computation.5 | async-start | bytes 983040 | tf_op jit(solution)/shard_map/reduce_scatter | solution.py:80
Sparse Core Ops, SparseCore 0:
  25.6 32.2 all-gather.4
  59.8 32.2 all-gather.2
  224.4 61.5 reduce-scatter.2
  288.3 23.3 reduce-scatter.4
where the time goes:
time: 321 us; the launch traced here: 320 us
  blocking collectives  133 us (41%)
  matrix products  95.6 us (30%)
  waiting for transfers between devices  61.1 us (19%)
  between operations  15.2 us (5%)
  local copies, waits for them, and re-layouts  8.11 us (3%)
  other arithmetic  7.1 us (2%)
    reduce_scatter x1, waiting for transfers between devices, shards(): lax.psum_scatter(lax.dot_general(grad_q, learn_head, (((1,), (1,)), ((),...  61 us
    psum x1, blocking collectives, shards(): lax.psum((learn_scaled, target_scaled, picked_part), ('dp', 'tensor'))  41.2 us
    pmax x1, blocking collectives, shards(): lax.pmax((learn_peak, target_peak), ('dp', 'tensor'))  38.1 us
    dot_general x1, matrix products, shards(): lax.dot_general(learn_all, grad_q, (((0,), (0,)), ((), ())), preferred_el...  26.1 us
    dot_general x1, matrix products, shards(): lax.dot_general(grad_q, learn_head, (((1,), (1,)), ((), ())), preferred_e...  23.8 us
    dot_general x1, matrix products, shards(): learn_q = jnp.dot(learn_all, learn_head, preferred_element_type=jnp.float32)  23.2 us
    dot_general x1, matrix products, shards(): jnp.dot(lax.all_gather(target_feat, 'dp', axis=0, tiled=True), target_hea...  22.3 us
    unnamed x2, blocking collectives  19.9 us
  transfers between devices with their start and end apart: 4, of which 1 were waited for; matrix products, arithmetic and copies ran while one was open for 17% of the time, Pallas kernels for 0%

commit v1 on v0

v1 whole, which is shorter than its diff:
```python
import functools

import jax
import jax.numpy as jnp
from jax import lax
from jax.experimental import pallas as pl
from jax.experimental.pallas import tpu as pltpu
from jax.sharding import PartitionSpec as P

temper = 1.0
discount = 0.99
kl_weight = 10.0
MESH = pl.DeviceIdType.MESH
SEMS = pltpu.SemaphoreType.DMA


def greet(dp, tp, me, slab):
    barrier = pltpu.get_barrier_semaphore()
    for d in range(1, dp):
        pl.semaphore_signal(
            barrier, inc=1, device_id={"dp": lax.rem(me + d, dp)}, device_id_type=MESH
        )
    for d in range(1, tp):
        pl.semaphore_signal(
            barrier, inc=1, device_id={"tensor": lax.rem(slab + d, tp)}, device_id_type=MESH
        )
    pl.semaphore_wait(barrier, dp - 1 + tp - 1)


def remote(src, dst, send, recv, device):
    return pltpu.make_async_remote_copy(
        src_ref=src,
        dst_ref=dst,
        send_sem=send,
        recv_sem=recv,
        device_id=device,
        device_id_type=MESH,
    )


def gather_kernel(
    dp, tp, learn, target, small, learn_out, target_out, small_out,
    own_sem, z_send, z_recv, p_send, p_recv, c_send, c_recv, s_send, s_recv,
):
    me, slab = lax.axis_index("dp"), lax.axis_index("tensor")
    chips = dp // 2
    chip, core = me // 2, lax.rem(me, 2)
    width = learn.shape[1]
    pairs = ((learn, learn_out), (target, target_out))

    def cols(j):
        return pl.ds(pl.multiple_of(lax.rem(slab + tp - j, tp) * width, width), width)

    greet(dp, tp, me, slab)
    own = []
    for a, (x, out) in enumerate(pairs):
        own.append(pltpu.make_async_copy(x, out.at[chip, core, :, cols(0)], own_sem.at[a]))
    own.append(pltpu.make_async_copy(small, small_out.at[me], own_sem.at[2]))
    for copy in own:
        copy.start()
    sent, z, p, c, s = [], {}, {}, {}, []
    for d in range(1, dp):
        copy = remote(
            small, small_out.at[me], s_send.at[d - 1], s_recv.at[d - 1],
            {"dp": lax.rem(me + d, dp)},
        )
        copy.start()
        s.append(copy)
    for a, (x, out) in enumerate(pairs):
        for d in range(1, tp):
            z[a, d] = remote(
                x, out.at[chip, core, :, cols(0)], z_send.at[a, d - 1], z_recv.at[a, d - 1],
                {"tensor": lax.rem(slab + d, tp)},
            )
            z[a, d].start()
    for a, (x, out) in enumerate(pairs):
        for j in range(tp):
            if j:
                z[a, j].wait_recv()
            place = out.at[chip, core, :, cols(j)]
            for d in range(1, chips):
                p[a, j, d] = remote(
                    x if j == 0 else place, place, p_send.at[a, j, d - 1], p_recv.at[a, j, d - 1],
                    {"dp": lax.rem(chip + d, chips) * 2 + core},
                )
                p[a, j, d].start()
    for copy in own:
        copy.wait()
    for a, (x, out) in enumerate(pairs):
        for j in range(tp):
            for d in range(1, chips):
                p[a, j, d].wait_recv()
            place = out.at[:, core, :, cols(j)]
            c[a, j] = remote(
                place, place, c_send.at[a, j], c_recv.at[a, j], {"dp": chip * 2 + 1 - core}
            )
            c[a, j].start()
    for copy in s:
        copy.wait_recv()
    for copy in c.values():
        copy.wait_recv()
    for copy in [*s, *z.values(), *p.values(), *c.values()]:
        copy.wait_send()


def gather(dp, tp, learn, target, small):
    rows, width = learn.shape
    chips = dp // 2
    full = jax.ShapeDtypeStruct((chips, 2, rows, tp * width), learn.dtype)
    return pl.pallas_call(
        functools.partial(gather_kernel, dp, tp),
        out_shape=(full, full, jax.ShapeDtypeStruct((dp, *small.shape), small.dtype)),
        in_specs=[pl.BlockSpec(memory_space=pl.ANY)] * 3,
        out_specs=(pl.BlockSpec(memory_space=pl.ANY),) * 3,
        scratch_shapes=[
            SEMS((3,)),
            SEMS((2, tp - 1)),
            SEMS((2, tp - 1)),
            SEMS((2, tp, chips - 1)),
            SEMS((2, tp, chips - 1)),
            SEMS((2, tp)),
            SEMS((2, tp)),
            SEMS((dp - 1,)),
            SEMS((dp - 1,)),
        ],
        compiler_params=pltpu.CompilerParams(collective_id=0, has_side_effects=True),
        name="gather_hidden",
    )(learn, target, small)


def combine(buffer, count):
    parts = [buffer[i] for i in range(count)]
    rows = []
    for top in (0, 2):
        peak = parts[0][top : top + 1]
        for part in parts[1:]:
            peak = jnp.maximum(peak, part[top : top + 1])
        total = jnp.zeros_like(peak)
        for part in parts:
            total += part[top + 1 : top + 2] * jnp.exp((part[top : top + 1] - peak) / temper)
        rows += [peak, total]
    picked = jnp.zeros_like(rows[0])
    for part in parts:
        picked += part[4:5]
    rows.append(picked)
    return jnp.concatenate(rows + [jnp.zeros_like(picked)] * 3, axis=0)


def stats_kernel(dp, tp, x, out, zbuf, dbuf, z_send, z_recv, d_send, d_recv):
    me, slab = lax.axis_index("dp"), lax.axis_index("tensor")
    greet(dp, tp, me, slab)
    copies = []
    for d in range(1, tp):
        copies.append(remote(
            x, zbuf.at[slab], z_send.at[d - 1], z_recv.at[d - 1],
            {"tensor": lax.rem(slab + d, tp)},
        ))
        copies[-1].start()
    zbuf[slab] = x[...]
    for copy in copies:
        copy.wait()
    dbuf[me] = combine(zbuf, tp)
    copies = []
    for d in range(1, dp):
        copies.append(remote(
            dbuf.at[me], dbuf.at[me], d_send.at[d - 1], d_recv.at[d - 1],
            {"dp": lax.rem(me + d, dp)},
        ))
        copies[-1].start()
    for copy in copies:
        copy.wait()
    out[...] = combine(dbuf, dp)


def merge_stats(dp, tp, stats):
    vmem = pl.BlockSpec(memory_space=pltpu.VMEM)
    return pl.pallas_call(
        functools.partial(stats_kernel, dp, tp),
        out_shape=jax.ShapeDtypeStruct(stats.shape, stats.dtype),
        in_specs=[vmem],
        out_specs=vmem,
        scratch_shapes=[
            pltpu.VMEM((tp, *stats.shape), stats.dtype),
            pltpu.VMEM((dp, *stats.shape), stats.dtype),
            SEMS((tp - 1,)),
            SEMS((tp - 1,)),
            SEMS((dp - 1,)),
            SEMS((dp - 1,)),
        ],
        compiler_params=pltpu.CompilerParams(collective_id=1, has_side_effects=True),
        name="merge_stats",
    )(stats)


def scatter_kernel(
    dp, tp, part, out, crecv, csum, precv, psum, zrecv,
    c_send, c_recv, p_send, p_recv, z_send, z_recv,
):
    me, slab = lax.axis_index("dp"), lax.axis_index("tensor")
    chips = dp // 2
    chip, core = me // 2, lax.rem(me, 2)
    width = out.shape[1]

    def owner(j):
        return lax.rem(slab + 1 + j, tp)

    def cols(j):
        return pl.ds(pl.multiple_of(owner(j) * width, width), width)

    greet(dp, tp, me, slab)
    c, p, z = [], {}, []
    for j in range(tp):
        c.append(remote(
            part.at[:, 1 - core, :, cols(j)], crecv.at[:, :, cols(j)],
            c_send.at[j], c_recv.at[j], {"dp": chip * 2 + 1 - core},
        ))
        c[-1].start()
    for j in range(tp):
        c[j].wait_recv()
        for g in range(chips):
            csum[g, :, cols(j)] = (
                part[g, core, :, cols(j)].astype(jnp.float32)
                + crecv[g, :, cols(j)].astype(jnp.float32)
            ).astype(csum.dtype)
        for d in range(1, chips):
            there = lax.rem(chip + d, chips)
            p[j, d] = remote(
                csum.at[there, :, cols(j)], precv.at[d - 1, :, cols(j)],
                p_send.at[j, d - 1], p_recv.at[j, d - 1], {"dp": there * 2 + core},
            )
            p[j, d].start()
    for j in range(tp):
        total = csum[chip, :, cols(j)].astype(jnp.float32)
        for d in range(1, chips):
            p[j, d].wait_recv()
            total += precv[d - 1, :, cols(j)].astype(jnp.float32)
        if j < tp - 1:
            psum[j] = total.astype(psum.dtype)
            z.append(remote(
                psum.at[j], zrecv.at[j], z_send.at[j], z_recv.at[j], {"tensor": owner(j)}
            ))
            z[-1].start()
    for j in range(tp - 1):
        z[j].wait_recv()
        total += zrecv[j].astype(jnp.float32)
    out[...] = total.astype(out.dtype)
    for copy in [*c, *p.values(), *z]:
        copy.wait_send()


def scatter_sum(dp, tp, part):
    chips, _, rows, features = part.shape
    width = features // tp
    vmem = pl.BlockSpec(memory_space=pltpu.VMEM)
    return pl.pallas_call(
        functools.partial(scatter_kernel, dp, tp),
        out_shape=jax.ShapeDtypeStruct((rows, width), part.dtype),
        in_specs=[vmem],
        out_specs=vmem,
        scratch_shapes=[
            pltpu.VMEM((chips, rows, features), part.dtype),
            pltpu.VMEM((chips, rows, features), part.dtype),
            pltpu.VMEM((chips - 1, rows, features), part.dtype),
            pltpu.VMEM((tp - 1, rows, width), part.dtype),
            pltpu.VMEM((tp - 1, rows, width), part.dtype),
            SEMS((tp,)),
            SEMS((tp,)),
            SEMS((tp, chips - 1)),
            SEMS((tp, chips - 1)),
            SEMS((tp - 1,)),
            SEMS((tp - 1,)),
        ],
        compiler_params=pltpu.CompilerParams(
            collective_id=2, has_side_effects=True, vmem_limit_bytes=40 * 1024 * 1024
        ),
        name="scatter_sum",
    )(part)


def local_stats(logits):
    row_max = jnp.max(logits, axis=1)
    total = jnp.sum(jnp.exp((logits - row_max[:, None]) / temper), axis=1)
    return (row_max, total)


def shards(dp, tp, learn_hidden, target_hidden, reward, learn_head, target_head, action, traj_len, owner):
    rows, width = learn_hidden.shape[0], learn_head.shape[1]
    tokens, features = rows * dp, learn_hidden.shape[1] * tp
    mine = traj_len.shape[0]
    traj_count = mine * dp
    seq_len = tokens // traj_count

    def row(x):
        x = x.astype(jnp.float32)
        return jnp.pad(x, (0, 128 - x.shape[0]))

    small = jnp.concatenate(
        [jnp.stack([row(action), row(reward), row(traj_len), row(owner)]), jnp.zeros((4, 128), jnp.float32)]
    )
    learn_all, target_all, small_all = gather(dp, tp, learn_hidden, target_hidden, small)
    learn_all = learn_all.reshape(tokens, features)
    target_all = target_all.reshape(tokens, features)
    action_all = small_all[:, 0, :rows].reshape(tokens).astype(jnp.int32)
    reward_all = small_all[:, 1, :rows].reshape(tokens)
    length_all = small_all[:, 2, :mine].reshape(traj_count).astype(jnp.int32)
    owner_all = small_all[:, 3, :mine].reshape(traj_count).astype(jnp.int32)

    learn_q = jnp.dot(learn_all, learn_head, preferred_element_type=jnp.float32)
    target_q = jnp.dot(target_all, target_head, preferred_element_type=jnp.float32)
    block_index = lax.axis_index("dp") * tp + lax.axis_index("tensor")
    columns = block_index * width + jnp.arange(width, dtype=jnp.int32)
    hits = action_all[:, None] == columns[None, :]
    picked_part = jnp.sum(jnp.where(hits, learn_q, 0.0), axis=1)
    learn_peak, learn_part = local_stats(learn_q)
    target_peak, target_part = local_stats(target_q)
    blank = jnp.zeros_like(picked_part)
    merged = merge_stats(
        dp, tp,
        jnp.stack([learn_peak, learn_part, target_peak, target_part, picked_part, blank, blank, blank]),
    )
    learn_max, learn_sum, target_max, target_sum, picked = (merged[i] for i in range(5))
    target_value = target_max + temper * jnp.log(target_sum)
    learn_p = jnp.exp((learn_q - learn_max[:, None]) / temper) / learn_sum[:, None]
    target_p = jnp.exp((target_q - target_max[:, None]) / temper) / target_sum[:, None]
    position = jnp.arange(tokens, dtype=jnp.int32)
    offset = position % seq_len
    lengths = jnp.repeat(length_all, seq_len)
    live = (offset < lengths).astype(jnp.float32)
    follow = (offset + 1 < lengths).astype(jnp.float32)
    shifted = jnp.concatenate([target_value[1:], jnp.zeros((1,), jnp.float32)])
    target_y = reward_all + discount * follow * shifted
    delta = live * (picked - target_y)
    grad_q = (
        jnp.where(hits, delta[:, None], 0.0)
        + kl_weight * live[:, None] * (learn_p - target_p) / temper
    ) / traj_count
    grad_q = grad_q.astype(jnp.bfloat16)
    part = lax.dot_general(
        grad_q, learn_head, (((1,), (1,)), ((), ())), preferred_element_type=jnp.float32
    ).astype(jnp.bfloat16)
    hidden_grad = scatter_sum(dp, tp, part.reshape(dp // 2, 2, rows, features))
    head_grad = lax.dot_general(
        learn_all, grad_q, (((0,), (0,)), ((), ())), preferred_element_type=jnp.float32
    ).astype(jnp.bfloat16)
    magnitude = jnp.abs(delta).reshape(traj_count, seq_len)
    holds = (owner_all == lax.axis_index("dp")).astype(jnp.float32)
    priority = jnp.sum(holds[:, None] * magnitude, axis=0, keepdims=True)
    return (head_grad, hidden_grad, priority)


def solution(mesh):
    dp, tp = mesh.shape["dp"], mesh.shape["tensor"]
    return jax.shard_map(
        functools.partial(shards, dp, tp),
        mesh=mesh,
        in_specs=(
            P("dp", "tensor"),
            P("dp", "tensor"),
            P("dp"),
            P(None, ("dp", "tensor")),
            P(None, ("dp", "tensor")),
            P("dp"),
            P("dp"),
            P("dp"),
        ),
        out_specs=(P(None, ("dp", "tensor")), P("dp", "tensor"), P("dp", None)),
        check_vma=False,
    )
```

time: 321 us -> 188 us (0.59)
  blocking collectives: 133 us -> 0 us
  Pallas kernels: 0 us -> 79 us
  waiting for transfers between devices: 61.1 us -> 0 us
  between operations: 15.2 us -> 0.79 us
  local copies, waits for them, and re-layouts: 8.11 us -> 3.65 us
    pallas_call x0 -> x3, Pallas kernels: none -> 79 us  [the longest x1 44.4 us: gather(): pl.pallas_call(functools.partial(gather_kernel, dp, tp), out_shape=(full,...]
    reduce_scatter x2 -> x0, waiting for transfers between devices: 61 us -> none  [the longest x1 61 us: shards(): lax.psum_scatter(lax.dot_general(grad_q, learn_head, (((1,), (1,)), ((),...]
    psum x1 -> x0, blocking collectives: 41.2 us -> none  [shards(): lax.psum((learn_scaled, target_scaled, picked_part), ('dp', 'tensor'))]
    pmax x1 -> x0, blocking collectives: 38.1 us -> none  [shards(): lax.pmax((learn_peak, target_peak), ('dp', 'tensor'))]
    all_gather x2 -> x0, blocking collectives: 33.9 us -> none  [the longest x1 18.3 us: shards(): lax.all_gather(target_hidden, 'tensor', axis=1, tiled=True)]
    unnamed x2 -> x0, blocking collectives: 19.9 us -> none
    unnamed x13 -> x7, local copies, waits for them, and re-layouts: 7.25 us -> 0.65 us
    dot_general x2 -> x1, matrix products: 22.4 us -> 23.4 us  [shards(): jnp.dot(target_all, target_head, preferred_element_type=jnp.float32)]
  transfers between devices with their start and end apart: 4 -> 0, of which waited for: 1 -> 0; matrix products, arithmetic and copies ran while one was open for 17% -> 0% of each run, Pallas kernels for 0% -> 0%
where the time goes in v1:
time: 188 us
  matrix products  95.4 us (51%)
  Pallas kernels  79 us (42%)
  other arithmetic  9.25 us (5%)
  local copies, waits for them, and re-layouts  3.65 us (2%)
    pallas_call x1, Pallas kernels, gather(): pl.pallas_call(functools.partial(gather_kernel, dp, tp), out_shape=(full,...  44.4 us
    dot_general x1, matrix products, shards(): lax.dot_general(learn_all, grad_q, (((0,), (0,)), ((), ())), preferred_el...  28.1 us
    dot_general x1, matrix products, shards(): jnp.dot(target_all, target_head, preferred_element_type=jnp.float32)  23.4 us
    pallas_call x1, Pallas kernels, scatter_sum(): pl.pallas_call(functools.partial(scatter_kernel, dp, tp), out_shape=jax.S...  23.2 us
    dot_general x1, matrix products, shards(): learn_q = jnp.dot(learn_all, learn_head, preferred_element_type=jnp.float32)  22.3 us
    dot_general x1, matrix products, shards(): lax.dot_general(grad_q, learn_head, (((1,), (1,)), ((), ())), preferred_e...  21.5 us
    pallas_call x1, Pallas kernels, merge_stats(): pl.pallas_call(functools.partial(stats_kernel, dp, tp), out_shape=jax.Sha...  11.4 us
    reduce_sum x1, other arithmetic, shards(): picked_part = jnp.sum(jnp.where(hits, learn_q, 0.0), axis=1)  4.88 us

profile of v1, /device:TPU:0, one launch (start us, length us, event | category | flops | bytes accessed | tf_op | source)
XLA Modules:
  0.0 188.1 jit_solution(14731050378569496528)
XLA Ops:
  0.6 0.7 convert_element_type.62
  1.3 0.7 bitcast_convert_fusion
  2.0 0.7 convert_element_type.64
  2.6 0.7 convert_element_type.63
  3.3 0.6 concatenate.12.small
  3.9 44.4 %gather_hidden.1 = (bf16[4,2,48,4096]{3,2,1,0:T(8,128)(2,1)}, bf16[4,2,48,4096]{3,2,1,0:T(8,128)(2,1)}, f32[8,8,128]{2,1,0:T(8,128)}) custom-call(bf16[48,1024]{1,0:T(8,128)(2,1)} %learn.1, bf16[48,1024]{1,0:T(8,128)(2,1)} %target.1, f32[8,128]{1,0:T(8,128)} %concatenate.12.small), custom_call_target="tpu_custom_call" | custom-call | tf_op jit(solution)/shard_map/gather_hidden/pallas_call | solution.py:110
  48.3 0.0 copy-start.2
  48.3 23.4 %fusion.17 = (f32[384]{0:T(512)S(1)}, f32[384,4008]{0,1:T(8,128)}) fusion(bf16[384,4096]{1,0:T(8,128)(2,1)} %bitcast.25, bf16[4096,4008]{0,1:T(8,128)(2,1)} %param.12), kind=kOutput, calls=%fused_computation.46 | convolution fusion | flops 12609616896 | bytes 42137088 | tf_op jit(solution)/shard_map/dot_general | solution.py:309
  71.7 0.0 copy-done.2
  71.7 22.3 %fusion.16 = (f32[384]{0:T(512)S(1)}, f32[384,4008]{0,1:T(8,128)}) fusion(bf16[384,4096]{1,0:T(8,128)(2,1)S(1)} %bitcast.23, bf16[4096,4008]{0,1:T(8,128)(2,1)} %param.11), kind=kOutput, calls=%fused_computation.45 | convolution fusion | flops 12609616896 | bytes 42137088 | tf_op jit(solution)/shard_map/dot_general | solution.py:308
  94.1 0.0 copy-done.1
  94.1 0.1 convert_element_type.66
  94.2 4.9 %fusion = (f32[384]{0:T(512)S(1)}, f32[384]{0:T(512)S(1)}) fusion(f32[384,4008]{0,1:T(8,128)} %get-tuple-element.22, s32[384]{0:T(512)S(1)} %convert_element_type.66, s32[4008]{0:T(1024)S(1)} %iota_add_fusion, f32[384]{0:T(512)S(1)} %get-tuple-element.21), kind=kLoop, calls=%fused_computation.3 | loop fusion | flops 7694592 | bytes 6178464 | tf_op jit(solution)/shard_map/reduce_sum | solution.py:313
  99.1 1.0 exponential_reduce_fusion
  100.1 0.6 stack.47.x
  100.8 11.4 %merge_stats.1 = f32[8,384]{1,0:T(8,128)} custom-call(f32[8,384]{1,0:T(8,128)} %stack.47.x), custom_call_target="tpu_custom_call" | custom-call | tf_op jit(solution)/shard_map/merge_stats/pallas_call | solution.py:177
  112.2 0.9 slice_reduce_fusion.4
  113.1 0.1 slice.36
  113.2 0.1 reshape_squeeze.8
  113.3 0.1 convert_element_type.68
  113.4 0.1 broadcast_in_dim.31
  113.5 0.1 reshape.126
  113.6 0.1 pad_maximum_fusion
  113.6 28.1 %convolution_convert_fusion = bf16[4096,4008]{0,1:T(8,128)(2,1)} fusion(bf16[384,4096]{1,0:T(8,128)(2,1)S(1)} %bitcast.24, f32[384,4008]{0,1:T(8,128)} %get-tuple-element.24, f32[384,4008]{0,1:T(8,128)} %get-tuple-element.22, f32[384]{0:T(512)S(1)} %get-tuple-element.14, f32[384]{0:T(512)S(1)} %get-tuple-element.15, f32[384]{0:T(512)S(1)} %get-tuple-element.12, ...), kind=kOutput, calls=%fused_computation | convolution fusion | flops 12641424384 | bytes 48318624 | tf_op jit(solution)/shard_map/dot_general | solution.py:342
  141.7 21.5 %convolution_convert_fusion.1 = bf16[384,4096]{1,0:T(8,128)(2,1)S(1)} fusion(bf16[4096,4008]{0,1:T(8,128)(2,1)} %param.11, f32[384,4008]{0,1:T(8,128)} %get-tuple-element.24, f32[384,4008]{0,1:T(8,128)} %get-tuple-element.22, f32[384]{0:T(512)S(1)} %get-tuple-element.14, f32[384]{0:T(512)S(1)} %get-tuple-element.15, f32[384]{0:T(512)S(1)} %get-tuple-element.12, ...), kind=kOutput, calls=%fused_computation.9 | convolution fusion | flops 12626580480 | bytes 48318624 | tf_op jit(solution)/shard_map/dot_general | solution.py:338
  163.2 23.2 %scatter_sum.1 = bf16[48,1024]{1,0:T(8,128)(2,1)S(1)} custom-call(bf16[4,2,48,4096]{3,2,1,0:T(8,128)(2,1)S(1)} %bitcast.20), custom_call_target="tpu_custom_call" | custom-call | tf_op jit(solution)/shard_map/scatter_sum/pallas_call | solution.py:255
  186.4 0.1 squeeze.14
  186.5 0.1 reshape_squeeze.9
  186.6 0.1 concatenate.14
  186.7 0.1 reshape.130
  186.8 0.6 multiply_reduce_fusion
  187.4 0.6 copy.12
  (19 shorter events, 0.1 us)
Async XLA Ops:
  48.3 23.4 %copy-start.2 = (bf16[4,2,48,4096]{3,2,1,0:T(8,128)(2,1)S(1)}, bf16[4,2,48,4096]{3,2,1,0:T(8,128)(2,1)}, u32[]{:S(2)}) copy-start(bf16[4,2,48,4096]{3,2,1,0:T(8,128)(2,1)} %get-tuple-element.6) | copy-start | bytes 9437188
  71.7 22.4 %copy-start.1 = (f32[8,8,128]{2,1,0:T(8,128)S(1)}, f32[8,8,128]{2,1,0:T(8,128)}, u32[]{:S(2)}) copy-start(f32[8,8,128]{2,1,0:T(8,128)} %get-tuple-element.7) | copy-start | bytes 98308
  94.2 4.9 %copy-start = (f32[384,4008]{0,1:T(8,128)S(1)}, f32[384,4008]{0,1:T(8,128)}, u32[]{:S(2)}) copy-start(f32[384,4008]{0,1:T(8,128)} %get-tuple-element.24) | copy-start | bytes 18468868

commit v2 on v1

--- a/solution.py
+++ b/solution.py
@@ -47,6 +47,7 @@
     chip, core = me // 2, lax.rem(me, 2)
     width = learn.shape[1]
     pairs = ((learn, learn_out), (target, target_out))
+    places = (learn_out.at[chip, core], target_out)
 
     def cols(j):
         return pl.ds(pl.multiple_of(lax.rem(slab + tp - j, tp) * width, width), width)
@@ -54,7 +55,7 @@
     greet(dp, tp, me, slab)
     own = []
     for a, (x, out) in enumerate(pairs):
-        own.append(pltpu.make_async_copy(x, out.at[chip, core, :, cols(0)], own_sem.at[a]))
+        own.append(pltpu.make_async_copy(x, places[a].at[:, cols(0)], own_sem.at[a]))
     own.append(pltpu.make_async_copy(small, small_out.at[me], own_sem.at[2]))
     for copy in own:
         copy.start()
@@ -69,7 +70,7 @@
     for a, (x, out) in enumerate(pairs):
         for d in range(1, tp):
             z[a, d] = remote(
-                x, out.at[chip, core, :, cols(0)], z_send.at[a, d - 1], z_recv.at[a, d - 1],
+                x, places[a].at[:, cols(0)], z_send.at[a, d - 1], z_recv.at[a, d - 1],
                 {"tensor": lax.rem(slab + d, tp)},
             )
             z[a, d].start()
@@ -77,8 +78,8 @@
         for j in range(tp):
             if j:
                 z[a, j].wait_recv()
-            place = out.at[chip, core, :, cols(j)]
-            for d in range(1, chips):
+            place = places[a].at[:, cols(j)]
+            for d in range(1, chips if a == 0 else 1):
                 p[a, j, d] = remote(
                     x if j == 0 else place, place, p_send.at[a, j, d - 1], p_recv.at[a, j, d - 1],
                     {"dp": lax.rem(chip + d, chips) * 2 + core},
@@ -86,7 +87,7 @@
                 p[a, j, d].start()
     for copy in own:
         copy.wait()
-    for a, (x, out) in enumerate(pairs):
+    for a, (x, out) in enumerate(pairs[:1]):
         for j in range(tp):
             for d in range(1, chips):
                 p[a, j, d].wait_recv()
@@ -107,19 +108,20 @@
     rows, width = learn.shape
     chips = dp // 2
     full = jax.ShapeDtypeStruct((chips, 2, rows, tp * width), learn.dtype)
+    line = jax.ShapeDtypeStruct((rows, tp * width), target.dtype)
     return pl.pallas_call(
         functools.partial(gather_kernel, dp, tp),
-        out_shape=(full, full, jax.ShapeDtypeStruct((dp, *small.shape), small.dtype)),
+        out_shape=(full, line, jax.ShapeDtypeStruct((dp, *small.shape), small.dtype)),
         in_specs=[pl.BlockSpec(memory_space=pl.ANY)] * 3,
         out_specs=(pl.BlockSpec(memory_space=pl.ANY),) * 3,
         scratch_shapes=[
             SEMS((3,)),
             SEMS((2, tp - 1)),
             SEMS((2, tp - 1)),
-            SEMS((2, tp, chips - 1)),
-            SEMS((2, tp, chips - 1)),
-            SEMS((2, tp)),
-            SEMS((2, tp)),
+            SEMS((1, tp, chips - 1)),
+            SEMS((1, tp, chips - 1)),
+            SEMS((1, tp)),
+            SEMS((1, tp)),
             SEMS((dp - 1,)),
             SEMS((dp - 1,)),
         ],
@@ -192,59 +194,57 @@
     )(stats)
 
 
-def scatter_kernel(
-    dp, tp, part, out, crecv, csum, precv, psum, zrecv,
-    c_send, c_recv, p_send, p_recv, z_send, z_recv,
-):
+def cores_kernel(dp, tp, part, *refs):
+    chips = dp // 2
+    outs, (crecv, c_send, c_recv) = refs[:chips], refs[chips:]
     me, slab = lax.axis_index("dp"), lax.axis_index("tensor")
-    chips = dp // 2
     chip, core = me // 2, lax.rem(me, 2)
-    width = out.shape[1]
-
-    def owner(j):
-        return lax.rem(slab + 1 + j, tp)
-
-    def cols(j):
-        return pl.ds(pl.multiple_of(owner(j) * width, width), width)
-
+    width = part.shape[3] // tp
     greet(dp, tp, me, slab)
-    c, p, z = [], {}, []
+    c = []
     for j in range(tp):
+        cols = pl.ds(j * width, width)
         c.append(remote(
-            part.at[:, 1 - core, :, cols(j)], crecv.at[:, :, cols(j)],
+            part.at[:, 1 - core, :, cols], crecv.at[:, :, cols],
             c_send.at[j], c_recv.at[j], {"dp": chip * 2 + 1 - core},
         ))
         c[-1].start()
     for j in range(tp):
         c[j].wait_recv()
-        for g in range(chips):
-            csum[g, :, cols(j)] = (
-                part[g, core, :, cols(j)].astype(jnp.float32)
-                + crecv[g, :, cols(j)].astype(jnp.float32)
-            ).astype(csum.dtype)
-        for d in range(1, chips):
-            there = lax.rem(chip + d, chips)
-            p[j, d] = remote(
-                csum.at[there, :, cols(j)], precv.at[d - 1, :, cols(j)],
-                p_send.at[j, d - 1], p_recv.at[j, d - 1], {"dp": there * 2 + core},
-            )
-            p[j, d].start()
+        cols = pl.ds(j * width, width)
+        for d in range(chips):
+            g = lax.rem(chip + d, chips)
+            outs[d][:, cols] = (
+                part[g, core, :, cols].astype(jnp.float32) + crecv[g, :, cols].astype(jnp.float32)
+            ).astype(outs[d].dtype)
+    for copy in c:
+        copy.wait_send()
+
+
+def slabs_kernel(dp, tp, *refs):
+    chips = dp // 2
+    parts, (out, psum, zrecv, z_send, z_recv) = refs[:chips], refs[chips:]
+    me, slab = lax.axis_index("dp"), lax.axis_index("tensor")
+    width = out.shape[1]
+    greet(dp, tp, me, slab)
+    z = []
     for j in range(tp):
-        total = csum[chip, :, cols(j)].astype(jnp.float32)
-        for d in range(1, chips):
-            p[j, d].wait_recv()
-            total += precv[d - 1, :, cols(j)].astype(jnp.float32)
+        owner = lax.rem(slab + 1 + j, tp)
+        cols = pl.ds(pl.multiple_of(owner * width, width), width)
+        total = parts[0][:, cols].astype(jnp.float32)
+        for part in parts[1:]:
+            total += part[:, cols].astype(jnp.float32)
         if j < tp - 1:
             psum[j] = total.astype(psum.dtype)
             z.append(remote(
-                psum.at[j], zrecv.at[j], z_send.at[j], z_recv.at[j], {"tensor": owner(j)}
+                psum.at[j], zrecv.at[j], z_send.at[j], z_recv.at[j], {"tensor": owner}
             ))
             z[-1].start()
     for j in range(tp - 1):
         z[j].wait_recv()
         total += zrecv[j].astype(jnp.float32)
     out[...] = total.astype(out.dtype)
-    for copy in [*c, *p.values(), *z]:
+    for copy in z:
         copy.wait_send()
 
 
@@ -252,29 +252,41 @@
     chips, _, rows, features = part.shape
     width = features // tp
     vmem = pl.BlockSpec(memory_space=pltpu.VMEM)
+    sums = pl.pallas_call(
+        functools.partial(cores_kernel, dp, tp),
+        out_shape=(jax.ShapeDtypeStruct((rows, features), part.dtype),) * chips,
+        in_specs=[vmem],
+        out_specs=(vmem,) * chips,
+        scratch_shapes=[
+            pltpu.VMEM((chips, rows, features), part.dtype),
+            SEMS((tp,)),
+            SEMS((tp,)),
+        ],
+        compiler_params=pltpu.CompilerParams(
+            collective_id=2, has_side_effects=True, vmem_limit_bytes=40 * 1024 * 1024
+        ),
+        name="sum_cores",
+    )(part)
+    arrived = [sums[0]]
+    for d in range(1, chips):
+        route = [(i, ((i // 2 + d) % chips) * 2 + i % 2) for i in range(dp)]
+        arrived.append(lax.ppermute(sums[d], "dp", route))
     return pl.pallas_call(
-        functools.partial(scatter_kernel, dp, tp),
+        functools.partial(slabs_kernel, dp, tp),
         out_shape=jax.ShapeDtypeStruct((rows, width), part.dtype),
-        in_specs=[vmem],
+        in_specs=[vmem] * chips,
         out_specs=vmem,
         scratch_shapes=[
-            pltpu.VMEM((chips, rows, features), part.dtype),
-            pltpu.VMEM((chips, rows, features), part.dtype),
-            pltpu.VMEM((chips - 1, rows, features), part.dtype),
             pltpu.VMEM((tp - 1, rows, width), part.dtype),
             pltpu.VMEM((tp - 1, rows, width), part.dtype),
-            SEMS((tp,)),
-            SEMS((tp,)),
-            SEMS((tp, chips - 1)),
-            SEMS((tp, chips - 1)),
             SEMS((tp - 1,)),
             SEMS((tp - 1,)),
         ],
         compiler_params=pltpu.CompilerParams(
-            collective_id=2, has_side_effects=True, vmem_limit_bytes=40 * 1024 * 1024
+            collective_id=3, has_side_effects=True, vmem_limit_bytes=40 * 1024 * 1024
         ),
-        name="scatter_sum",
-    )(part)
+        name="sum_slabs",
+    )(*arrived)
 
 
 def local_stats(logits):
@@ -299,7 +311,7 @@
     )
     learn_all, target_all, small_all = gather(dp, tp, learn_hidden, target_hidden, small)
     learn_all = learn_all.reshape(tokens, features)
-    target_all = target_all.reshape(tokens, features)
+    target_all = lax.all_gather(target_all, "dp", axis=0, tiled=True)
     action_all = small_all[:, 0, :rows].reshape(tokens).astype(jnp.int32)
     reward_all = small_all[:, 1, :rows].reshape(tokens)
     length_all = small_all[:, 2, :mine].reshape(traj_count).astype(jnp.int32)

time: 188 us -> 189 us (level)
  Pallas kernels: 79 us -> 55.3 us
  between operations: 0.79 us -> 14.2 us
  waiting for transfers between devices: 0 us -> 5.93 us
  starting transfers between devices: 0 us -> 4.23 us
  local copies, waits for them, and re-layouts: 3.65 us -> 6.23 us
    pallas_call x1, Pallas kernels: 44.4 us -> 27.3 us  [gather(): pl.pallas_call(functools.partial(gather_kernel, dp, tp), out_shape=(full,...]
    pallas_call x1 -> x2, Pallas kernels: 23.2 us -> 16.6 us  [the longest x1 10.8 us: scatter_sum(): pl.pallas_call(functools.partial(slabs_kernel, dp, tp), out_shape=jax.Sha...]
    all_gather x0 -> x1, waiting for transfers between devices: none -> 5.9 us  [shards(): target_all = lax.all_gather(target_all, 'dp', axis=0, tiled=True)]
    ppermute x0 -> x3, starting transfers between devices: none -> 4.19 us  [scatter_sum(): arrived.append(lax.ppermute(sums[d], 'dp', route))]
    unnamed x7 -> x5, local copies, waits for them, and re-layouts: 0.65 us -> 3.23 us
  transfers between devices with their start and end apart: 0 -> 4, of which waited for: 0 -> 1; matrix products, arithmetic and copies ran while one was open for 0% -> 30% of each run, Pallas kernels for 0% -> 0%
where the time goes in v2:
time: 189 us
  matrix products  93.8 us (50%)
  Pallas kernels  55.3 us (29%)
  between operations  14.2 us (8%)
  other arithmetic  8.82 us (5%)
  local copies, waits for them, and re-layouts  6.23 us (3%)
  waiting for transfers between devices  5.93 us (3%)
  starting transfers between devices  4.23 us (2%)
    pallas_call x1, Pallas kernels, gather(): pl.pallas_call(functools.partial(gather_kernel, dp, tp), out_shape=(full,...  27.3 us
    dot_general x1, matrix products, shards(): lax.dot_general(learn_all, grad_q, (((0,), (0,)), ((), ())), preferred_el...  26.7 us
    dot_general x1, matrix products, shards(): learn_q = jnp.dot(learn_all, learn_head, preferred_element_type=jnp.float32)  23.3 us
    dot_general x1, matrix products, shards(): jnp.dot(target_all, target_head, preferred_element_type=jnp.float32)  22.2 us
    dot_general x1, matrix products, shards(): lax.dot_general(grad_q, learn_head, (((1,), (1,)), ((), ())), preferred_e...  21.6 us
    pallas_call x1, Pallas kernels, merge_stats(): pl.pallas_call(functools.partial(stats_kernel, dp, tp), out_shape=jax.Sha...  11.4 us
    pallas_call x1, Pallas kernels, scatter_sum(): pl.pallas_call(functools.partial(slabs_kernel, dp, tp), out_shape=jax.Sha...  10.8 us
    all_gather x1, waiting for transfers between devices, shards(): target_all = lax.all_gather(target_all, 'dp', axis=0, tiled=True)  5.9 us
  transfers between devices with their start and end apart: 4, of which 1 were waited for; matrix products, arithmetic and copies ran while one was open for 30% of the time, Pallas kernels for 0%

profile of v2, /device:TPU:0, one launch (start us, length us, event | category | flops | bytes accessed | tf_op | source)
XLA Modules:
  0.0 188.5 jit_solution(7790834868746423975)
XLA Ops:
  7.2 0.7 convert_element_type.62
  7.9 0.7 bitcast_convert_fusion
  8.5 0.7 convert_element_type.64
  9.2 0.7 convert_element_type.63
  9.9 0.6 concatenate.12.small
  10.5 27.3 %gather_hidden.1 = (bf16[4,2,48,4096]{3,2,1,0:T(8,128)(2,1)}, bf16[48,4096]{1,0:T(8,128)(2,1)}, f32[8,8,128]{2,1,0:T(8,128)}) custom-call(bf16[48,1024]{1,0:T(8,128)(2,1)} %learn.1, bf16[48,1024]{1,0:T(8,128)(2,1)} %target.1, f32[8,128]{1,0:T(8,128)} %concatenate.12.small), custom_call_target="tpu_custom_call" | custom-call | tf_op jit(solution)/shard_map/gather_hidden/pallas_call | solution.py:112
  37.8 23.3 %fusion.16 = (f32[384]{0:T(512)S(1)}, f32[384,4008]{0,1:T(8,128)}) fusion(bf16[384,4096]{1,0:T(8,128)(2,1)} %bitcast.22, bf16[4096,4008]{0,1:T(8,128)(2,1)} %param.11), kind=kOutput, calls=%fused_computation.45 | convolution fusion | flops 12609616896 | bytes 42137088 | tf_op jit(solution)/shard_map/dot_general | solution.py:320
  61.1 0.1 convert_element_type.66
  61.2 4.5 %fusion = (f32[384]{0:T(512)S(1)}, f32[384]{0:T(512)S(1)}) fusion(f32[384,4008]{0,1:T(8,128)} %get-tuple-element.30, s32[384]{0:T(512)S(1)} %convert_element_type.66, s32[4008]{0:T(1024)S(1)} %iota_add_fusion, f32[384]{0:T(512)S(1)} %get-tuple-element.29), kind=kLoop, calls=%fused_computation.3 | loop fusion | flops 7694592 | bytes 6178464 | tf_op jit(solution)/shard_map/reduce_sum | solution.py:325
  65.7 0.1 reshape_squeeze.8
  65.8 0.1 convert_element_type.68
  66.0 0.1 reshape.123
  66.1 0.1 reshape.126
  66.2 5.9 %all-gather.2.cloned.1.call-done = bf16[384,4096]{1,0:T(8,128)(2,1)} async-done(((bf16[48,4096]{1,0:T(8,128)(2,1)}), bf16[384,4096]{1,0:T(8,128)(2,1)}) %all-gather.2.cloned.1.call-update) | async-done | bytes 3145744 | tf_op jit(solution)/shard_map/all_gather | solution.py:314
  72.1 22.2 %fusion.17 = (f32[384]{0:T(512)S(1)}, f32[384,4008]{0,1:T(8,128)S(1)}) fusion(bf16[384,4096]{1,0:T(8,128)(2,1)} %all-gather.2.cloned.1.call-done, bf16[4096,4008]{0,1:T(8,128)(2,1)} %param.12), kind=kOutput, calls=%fused_computation.46 | convolution fusion | flops 12609616896 | bytes 42137088 | tf_op jit(solution)/shard_map/dot_general | solution.py:321
  94.4 2.6 %copy-done = f32[384,4008]{0,1:T(8,128)} copy-done((f32[384,4008]{0,1:T(8,128)}, f32[384,4008]{0,1:T(8,128)S(1)}, u32[]{:S(2)}) %copy-start) | copy-done | bytes 6156312
  96.9 1.0 exponential_reduce_fusion
  97.9 0.6 stack.47.x
  98.6 11.4 %merge_stats.1 = f32[8,384]{1,0:T(8,128)} custom-call(f32[8,384]{1,0:T(8,128)} %stack.47.x), custom_call_target="tpu_custom_call" | custom-call | tf_op jit(solution)/shard_map/merge_stats/pallas_call | solution.py:179
  110.0 0.9 slice_reduce_fusion.4
  111.0 0.1 pad_maximum_fusion
  111.1 21.6 %convolution_convert_fusion.1 = bf16[384,4096]{1,0:T(8,128)(2,1)S(1)} fusion(bf16[4096,4008]{0,1:T(8,128)(2,1)} %param.11, f32[384,4008]{0,1:T(8,128)} %copy-done, f32[384,4008]{0,1:T(8,128)} %get-tuple-element.30, f32[384]{0:T(512)S(1)} %get-tuple-element.22, f32[384]{0:T(512)S(1)} %get-tuple-element.23, f32[384]{0:T(512)S(1)} %get-tuple-element.20, ...), kind=kOutput, calls=%fused_computation.9 | convolution fusion | flops 12626580480 | bytes 48318624 | tf_op jit(solution)/shard_map/dot_general | solution.py:350
  132.7 5.8 %sum_cores.1 = (bf16[48,4096]{1,0:T(8,128)(2,1)S(1)}, bf16[48,4096]{1,0:T(8,128)(2,1)S(1)}, bf16[48,4096]{1,0:T(8,128)(2,1)S(1)}, bf16[48,4096]{1,0:T(8,128)(2,1)S(1)}) custom-call(bf16[4,2,48,4096]{3,2,1,0:T(8,128)(2,1)S(1)} %bitcast.19), custom_call_target="tpu_custom_call" | custom-call | tf_op jit(solution)/shard_map/sum_cores/pallas_call | solution.py:255
  138.5 1.4 collective-permute-start
  140.0 0.7 collective-permute-start.1
  140.6 2.1 %collective-permute-start.2 = (bf16[48,4096]{1,0:T(8,128)(2,1)S(1)}, bf16[48,4096]{1,0:T(8,128)(2,1)S(1)}, u32[]{:S(2)}, u32[]{:S(2)}) collective-permute-start(bf16[48,4096]{1,0:T(8,128)(2,1)S(1)} %get-tuple-element.16), channel_id=1, source_target_pairs={{0,24},{4,28},{8,0},{12,4},{16,8},{20,12},{24,16},{28,20},{1,25},{... | collective-permute-start | bytes 1179656 | tf_op jit(solution)/shard_map/ppermute | solution.py:273
  142.7 26.7 %convolution_convert_fusion = bf16[4096,4008]{0,1:T(8,128)(2,1)} fusion(bf16[384,4096]{1,0:T(8,128)(2,1)} %bitcast.23, f32[384,4008]{0,1:T(8,128)} %copy-done, f32[384,4008]{0,1:T(8,128)} %get-tuple-element.30, f32[384]{0:T(512)S(1)} %get-tuple-element.22, f32[384]{0:T(512)S(1)} %get-tuple-element.23, f32[384]{0:T(512)S(1)} %get-tuple-element.20, ...), kind=kOutput, calls=%fused_computation | convolution fusion | flops 12641424384 | bytes 48318624 | tf_op jit(solution)/shard_map/dot_general | solution.py:354
  169.4 0.1 squeeze.14
  169.5 0.1 concatenate.14
  169.6 0.6 multiply_reduce_fusion
  170.2 10.8 %sum_slabs.1 = bf16[48,1024]{1,0:T(8,128)(2,1)S(1)} custom-call(bf16[48,4096]{1,0:T(8,128)(2,1)S(1)} %get-tuple-element.13.refs_0_, bf16[48,4096]{1,0:T(8,128)(2,1)S(1)} %collective-permute-done.refs_1_, bf16[48,4096]{1,0:T(8,128)(2,1)S(1)} %collective-permute-done.1.refs_2_, bf16[48,4096]{1,0:T(8,128)(2,1)S(1)} %collective-permute-done.2.refs_3_), custom_call_target="tpu_custom_call" | custom-call | tf_op jit(solution)/shard_map/sum_slabs/pallas_call | solution.py:274
  181.0 0.6 copy.12
  (27 shorter events, 0.4 us)
Async XLA Ops:
  7.2 65.0 %all-gather.2.cloned.1.call-start = ((), (), s32[]{:S(2)}) async-start(), calls=%async_computation | async-start | bytes 3538944 | tf_op jit(solution)/shard_map/all_gather | solution.py:314
  37.8 23.3 %copy-start.1 = (f32[8,8,128]{2,1,0:T(8,128)S(1)}, f32[8,8,128]{2,1,0:T(8,128)}, u32[]{:S(2)}) copy-start(f32[8,8,128]{2,1,0:T(8,128)} %get-tuple-element.11) | copy-start | bytes 98308
  94.3 2.6 %copy-start = (f32[384,4008]{0,1:T(8,128)}, f32[384,4008]{0,1:T(8,128)S(1)}, u32[]{:S(2)}) copy-start(f32[384,4008]{0,1:T(8,128)S(1)} %get-tuple-element.32) | copy-start | bytes 18468868
  138.5 31.6 %collective-permute-start = (bf16[48,4096]{1,0:T(8,128)(2,1)S(1)}, bf16[48,4096]{1,0:T(8,128)(2,1)S(1)}, u32[]{:S(2)}, u32[]{:S(2)}) collective-permute-start(bf16[48,4096]{1,0:T(8,128)(2,1)S(1)} %get-tuple-element.14), channel_id=1, source_target_pairs={{0,8},{4,12},{8,16},{12,20},{16,24},{20,28},{24,0},{28,4},{1,9},{5... | collective-permute-start | bytes 1179656 | tf_op jit(solution)/shard_map/ppermute | solution.py:273
  140.0 30.2 %collective-permute-start.1 = (bf16[48,4096]{1,0:T(8,128)(2,1)S(1)}, bf16[48,4096]{1,0:T(8,128)(2,1)S(1)}, u32[]{:S(2)}, u32[]{:S(2)}) collective-permute-start(bf16[48,4096]{1,0:T(8,128)(2,1)S(1)} %get-tuple-element.15), channel_id=1, source_target_pairs={{0,16},{4,20},{8,24},{12,28},{16,0},{20,4},{24,8},{28,12},{1,17},{... | collective-permute-start | bytes 1179656 | tf_op jit(solution)/shard_map/ppermute | solution.py:273
  140.6 29.6 %collective-permute-start.2 = (bf16[48,4096]{1,0:T(8,128)(2,1)S(1)}, bf16[48,4096]{1,0:T(8,128)(2,1)S(1)}, u32[]{:S(2)}, u32[]{:S(2)}) collective-permute-start(bf16[48,4096]{1,0:T(8,128)(2,1)S(1)} %get-tuple-element.16), channel_id=1, source_target_pairs={{0,24},{4,28},{8,0},{12,4},{16,8},{20,12},{24,16},{28,20},{1,25},{... | collective-permute-start | bytes 1179656 | tf_op jit(solution)/shard_map/ppermute | solution.py:273
Sparse Core Ops, SparseCore 0:
  37.9 34.2 all-gather.1
